TPU v7x, 128 devices: a whole 4x4x4 slice. The times are simulated.
128 devices in a mesh: seq: 8 (over z, core), enc: 16 (over x, y).
Axes of the slice: x: 4, y: 4, z: 4, core: 2. Of those that a mesh axis runs over, the one named last changes fastest.
Arguments:
- queries: bfloat16 [16384, 4096], P(('seq', 'enc')), may hold values from -8 to 8
- keys: bfloat16 [16, 1601, 512], P('enc'), may hold values from -8 to 8
- values: bfloat16 [16, 1601, 512], P('enc'), may hold values from -24 to 24
- reads: int32 [128, 8], replicated, may hold values from 0 to 15, all different within a row; in each aligned block of 16 rows (0 to 15, 16 to 31, ...) at most 12 rows name the same one
- grad_out: bfloat16 [16384, 4096], P(('seq', 'enc')), may hold values from -24 to 24
Outputs:
- attended: bfloat16 [16384, 4096], P(('seq', 'enc'))
- grad_queries: bfloat16 [16384, 4096], P(('seq', 'enc'))
- grad_keys: bfloat16 [16, 1601, 512], P('enc', None, 'seq')
- grad_values: bfloat16 [16, 1601, 512], P('enc', None, 'seq')
Inputs may be any that keep to these rules, and one draw needn't show every extreme that they name: `reads`: each row names 8 different images; in each aligned block of 16 rows (the text blocks of one index of seq) no image is named by more than 12 rows, and in some such block one image is named by exactly 12.
All inputs are finite; a program needn't handle non-finite values.
Results may differ from a plain program's by a relative error of at most 0.04.
Values may be sent and summed in bfloat16 or wider, within the bound.
A program may use at most 128 MiB of HBM per device.

v0:
```python
import functools

import jax
import jax.numpy as jnp
from jax import lax
from jax.experimental import pallas as pl
from jax.experimental.pallas import tpu as pltpu
from jax.sharding import PartitionSpec as P

HQ = 32
KVH = 4
HD = 128
GROUP = HQ // KVH
SEG = 16
ROWS = GROUP * SEG
VT = 1601
VT16 = 1616
JP = 1664
LOG2E = 1.4426950408889634
MESH = pl.DeviceIdType.MESH
BF16 = jnp.bfloat16
F32 = jnp.float32
CHUNKS = [(j, min(256, JP - j)) for j in range(0, JP, 256)]
NT = (((1,), (1,)), ((), ()))
T_SEND, T_SRC, T_OK, T_POS, T_READ = 0, 16, 32, 48, 64


def kernel(
    slots, tab, q_in, g_in, k_in, v_in, att_out, gq_out, gk_out, gv_out,
    a_q, a_g, a_o, a_d, m_q, m_g, m_o, m_d, r_q, r_g, r_o, r_d,
    kh, vh, kt, vt, stage_q, stage_g, pack_o, pack_d, s_scr, p_scr, k_acc, v_acc,
    z_send, z_recv, c_send, c_recv,
    s1, w1, s2, w2, zs, zw, cs, cw,
):
    sq = lax.axis_index("seq")
    en = lax.axis_index("enc")
    z, core = sq // 2, sq % 2
    x, y = en // 4, en % 4
    scale = HD ** (-0.5)

    first = (a_q, a_g, a_o, a_d)
    middle = (m_q, m_g, m_o, m_d)
    last = (r_q, r_g, r_o, r_d)
    own = [(x, y), (y, x), (x, y), (y, x)]

    def peer(axis, d):
        if axis == 0:
            return (sq, ((x + d) % 4) * 4 + y)
        return (sq, x * 4 + (y + d) % 4)

    def hop1(ten, t, d):
        return pltpu.make_async_remote_copy(
            src_ref=first[ten].at[t, d - 1],
            dst_ref=middle[ten].at[t, :, own[ten][0]],
            send_sem=s1.at[ten, t, d - 1],
            recv_sem=w1.at[ten, t, d - 1],
            device_id=peer(ten % 2, d),
            device_id_type=MESH,
        )

    def hop2(ten, t, d):
        b = own[ten][1]
        return pltpu.make_async_remote_copy(
            src_ref=middle[ten].at[t, (b + d) % 4],
            dst_ref=last[ten].at[t, b],
            send_sem=s2.at[ten, t, d - 1],
            recv_sem=w2.at[ten, t, d - 1],
            device_id=peer(1 - ten % 2, d),
            device_id_type=MESH,
        )

    def start1(pair, t):
        for d in (2, 1, 3):
            for ten in pair:
                hop1(ten, t, d).start()

    def forward(pair, t):
        for ten in pair:
            for d in (1, 2, 3):
                hop1(ten, t, d).wait_recv()
            for d in (2, 1, 3):
                hop2(ten, t, d).start()

    def arrive(pair, t):
        for ten in pair:
            for d in (1, 2, 3):
                hop2(ten, t, d).wait_recv()

    def z_copy(t):
        return pltpu.make_async_remote_copy(
            src_ref=z_send.at[t],
            dst_ref=z_recv.at[t],
            send_sem=zs.at[t],
            recv_sem=zw.at[t],
            device_id=(((z + 1 + t) % 4) * 2 + core, en),
            device_id_type=MESH,
        )

    def head_at(t):
        return (z + 1 + t) % 4

    IN, OUT = (0, 1), (2, 3)

    barrier = pltpu.get_barrier_semaphore()
    for d in (1, 2, 3):
        for target in (peer(0, d), peer(1, d), (((z + d) % 4) * 2 + core, en)):
            pl.semaphore_signal(barrier, inc=1, device_id=target, device_id_type=MESH)
    pl.semaphore_signal(barrier, inc=1, device_id=(z * 2 + 1 - core, en), device_id_type=MESH)

    def pack_in(t):
        cols = pl.ds(pl.multiple_of(head_at(t) * (GROUP * HD), GROUP * HD), GROUP * HD)
        for ten, src in ((0, q_in), (1, g_in)):
            a_own = own[ten][0]
            for d in range(4):
                a = (a_own + d) % 4
                for b in range(4):
                    image = a * 4 + b if ten == 0 else b * 4 + a
                    block = src[tab[T_SEND + image], :, cols]
                    for g in range(GROUP):
                        piece = block[:, g * HD : (g + 1) * HD]
                        rows = pl.ds(g * SEG, SEG)
                        if d == 0:
                            middle[ten][t, b, a_own, rows, :] = piece
                        else:
                            first[ten][t, d - 1, b, rows, :] = piece

    pack_in(0)
    pl.semaphore_wait(barrier, 10)
    start1(IN, 0)
    pack_in(1)
    start1(IN, 1)

    def rest(t, carry):
        pack_in(t)
        return carry

    lax.fori_loop(2, KVH, rest, 0)

    def heads(t, carry):
        cols = pl.ds(pl.multiple_of(head_at(t) * HD, HD), HD)
        for src, rows_ref, cols_ref in ((k_in, kh, kt), (v_in, vh, vt)):
            rows_ref[t, 0:1600, :] = src[0, 0:1600, cols]
            tail = src[0, 1600:VT, cols].astype(F32)
            mark = lax.broadcasted_iota(jnp.int32, (64, HD), 0) == 0
            rows_ref[t, 1600:JP, :] = jnp.where(
                mark, jnp.broadcast_to(tail, (64, HD)), 0.0
            ).astype(BF16)
            for j in range(0, JP, HD):
                cols_ref[t, :, j : j + HD] = rows_ref[t, j : j + HD, :].T
        return carry

    lax.fori_loop(0, KVH, heads, 0)

    forward(IN, 0)
    start1(IN, 2)

    def tile(t, i):
        src0, src1 = tab[T_SRC + 2 * i], tab[T_SRC + 2 * i + 1]
        ok0, ok1 = tab[T_OK + 2 * i], tab[T_OK + 2 * i + 1]
        turned0 = (src0 % 4) * 4 + src0 // 4
        turned1 = (src1 % 4) * 4 + src1 // 4
        q = jnp.concatenate([stage_q[turned0], stage_q[turned1]], axis=0)
        g0 = stage_g[src0].astype(F32)
        g1 = stage_g[src1].astype(F32)
        g_t = jnp.concatenate(
            [jnp.where(ok0 > 0, g0, 0.0).T, jnp.where(ok1 > 0, g1, 0.0).T], axis=1
        )
        top = jnp.full((8, 2 * ROWS), -jnp.inf, F32)
        for j, n in CHUNKS:
            s = lax.dot_general(kh[t, j : j + n, :], q, NT, preferred_element_type=F32)
            if j + n > VT:
                row = lax.broadcasted_iota(jnp.int32, s.shape, 0) + j
                s = jnp.where(row < VT, s, -1e30)
            s_scr[j : j + n, :] = s
            top = jnp.maximum(top, jnp.max(s.reshape(n // 8, 8, 2 * ROWS), axis=0))
        c2 = scale * LOG2E
        top2 = jnp.max(top, axis=0, keepdims=True) * c2
        total = jnp.zeros((8, 2 * ROWS), F32)
        o_t = jnp.zeros((HD, 2 * ROWS), F32)
        for j, n in CHUNKS:
            p = jnp.exp2(s_scr[j : j + n, :] * c2 - top2)
            total += jnp.sum(p.reshape(n // 8, 8, 2 * ROWS), axis=0)
            p_b = p.astype(BF16)
            p_scr[j : j + n, :] = p_b
            o_t += jnp.dot(vt[t, :, j : j + n], p_b, preferred_element_type=F32)
        inv = 1.0 / jnp.sum(total, axis=0, keepdims=True)
        o_t = (o_t * inv).astype(BF16).astype(F32)
        pack_o[2 * i] = o_t[:, :ROWS].T.astype(BF16)
        pack_o[2 * i + 1] = o_t[:, ROWS:].T.astype(BF16)
        delta = jnp.sum(g_t * o_t, axis=0, keepdims=True) * inv
        g_s = (g_t * inv).astype(BF16)
        d_t = jnp.zeros((HD, 2 * ROWS), F32)
        for j, n in CHUNKS:
            dp = jnp.dot(vh[t, j : j + n, :], g_s, preferred_element_type=F32)
            p_b = p_scr[j : j + n, :]
            ds = (p_b.astype(F32) * (dp - delta)).astype(BF16)
            v_acc[j : j + n, :] += lax.dot_general(p_b, g_s, NT, preferred_element_type=F32)
            k_acc[j : j + n, :] += jnp.dot(ds, q, preferred_element_type=F32)
            d_t += jnp.dot(kt[t, :, j : j + n], ds, preferred_element_type=F32)
        d_t = d_t * scale
        pack_d[2 * i] = d_t[:, :ROWS].T.astype(BF16)
        pack_d[2 * i + 1] = d_t[:, ROWS:].T.astype(BF16)

    def step(t, carry):
        arrive(IN, t)
        for ten, stage in ((0, stage_q), (1, stage_g)):
            b_own = own[ten][1]
            for d in range(4):
                b = (b_own + d) % 4
                for a in range(4):
                    if d == 0:
                        stage[b * 4 + a] = middle[ten][t, b, a]
                    else:
                        stage[b * 4 + a] = last[ten][t, b, a]
        k_acc[...] = jnp.zeros_like(k_acc)
        v_acc[...] = jnp.zeros_like(v_acc)

        def one(i, inner):
            tile(t, i)

            @pl.when((i == 0) & (t < KVH - 1))
            def _():
                forward(IN, t + 1)

            @pl.when((i == 0) & (t + 3 < KVH))
            def _():
                start1(IN, t + 3)

            @pl.when((i == 2) & (t > 0))
            def _():
                forward(OUT, t - 1)

            return inner

        lax.fori_loop(0, slots // 2, one, 0)

        for ten, packed in ((2, pack_o), (3, pack_d)):
            a_own = own[ten][0]
            for d in range(4):
                a = (a_own + d) % 4
                for b in range(4):
                    block = a * 4 + b if ten == 2 else b * 4 + a
                    piece = packed[tab[T_POS + block]]
                    if d == 0:
                        middle[ten][t, b, a_own] = piece
                    else:
                        first[ten][t, d - 1, b] = piece
        start1(OUT, t)

        @pl.when(t < KVH - 1)
        def _():
            z_send[t, 0] = (k_acc[0:VT16, :] * scale).astype(BF16)
            z_send[t, 1] = v_acc[0:VT16, :].astype(BF16)
            z_copy(t).start()

        return carry

    lax.fori_loop(0, KVH, step, 0)

    for t in range(KVH - 1):
        z_copy(t).wait_recv()

    def total_of(j, n):
        rows = pl.ds(j, n)
        sums = [k_acc[rows, :] * scale, v_acc[rows, :]]
        for t in range(KVH - 1):
            for w in (0, 1):
                sums[w] = sums[w] + z_recv[t, w, rows, :].astype(F32)
        return sums

    parts = [(j, min(256, VT16 - j)) for j in range(0, VT16, 256)]
    for j, n in parts:
        sums = total_of(j, n)
        rows = pl.ds(j, n)
        k_acc[rows, :] = sums[0]
        v_acc[rows, :] = sums[1]
        c_send[0, rows, :] = sums[0].astype(BF16)
        c_send[1, rows, :] = sums[1].astype(BF16)
    core_copy = pltpu.make_async_remote_copy(
        src_ref=c_send,
        dst_ref=c_recv,
        send_sem=cs,
        recv_sem=cw,
        device_id=(z * 2 + 1 - core, en),
        device_id_type=MESH,
    )
    core_copy.start()
    forward(OUT, KVH - 1)
    core_copy.wait_recv()
    for w, acc, out in ((0, k_acc, gk_out), (1, v_acc, gv_out)):
        for j, n in parts:
            full = acc[j : j + n, :] + c_recv[w, j : j + n, :].astype(F32)
            half = jnp.where(core == 0, full[:, 0:64], full[:, 64:128]).astype(BF16)
            if j + n > VT:
                out[0, j:1600, :] = half[0 : 1600 - j]
                out[0, 1600:VT, :] = half[1600 - j : VT - j]
            else:
                out[0, j : j + n, :] = half

    for t in range(KVH):
        arrive(OUT, t)

    def collect(t, carry):
        cols0 = head_at(t) * (GROUP * HD)
        for ten, out in ((2, att_out), (3, gq_out)):
            b_own = own[ten][1]
            for d in range(4):
                b = (b_own + d) % 4
                for a in range(4):
                    src = middle[ten] if d == 0 else last[ten]
                    stage = stage_q if ten == 2 else stage_g
                    stage[b * 4 + a] = src[t, b, a]
            for r in range(8):
                image = tab[T_READ + r]
                if ten == 2:
                    block = stage_q[(image % 4) * 4 + image // 4]
                else:
                    block = stage_g[image]
                for g in range(GROUP):
                    cols = pl.ds(pl.multiple_of(cols0 + g * HD, HD), HD)
                    out[r, :, cols] = block[g * SEG : (g + 1) * SEG, :]
        return carry

    lax.fori_loop(0, KVH, collect, 0)

    for t in range(KVH):
        for ten in range(4):
            for d in (1, 2, 3):
                hop1(ten, t, d).wait_send()
                hop2(ten, t, d).wait_send()
    for t in range(KVH - 1):
        z_copy(t).wait_send()
    core_copy.wait_send()


def tables(reads, slots):
    row = lax.axis_index("seq")
    own = lax.axis_index("enc")
    peers = 16
    row_reads = lax.dynamic_slice_in_dim(reads, row * peers, peers, 0)
    own_reads = lax.dynamic_index_in_dim(row_reads, own, 0, keepdims=False)
    ids = jnp.arange(16, dtype=jnp.int32)
    segs = jnp.arange(8, dtype=jnp.int32)
    send = jnp.sum(jnp.where(own_reads[None, :] == ids[:, None], segs[None, :], 0), axis=1)
    occupied = jnp.any(row_reads == own, axis=1)
    before = jnp.sum(
        jnp.where(occupied[None, :] & (ids[None, :] < ids[:, None]), 1, 0), axis=1
    )
    count = jnp.sum(jnp.where(occupied, 1, 0))
    place = (before[None, :] == ids[:, None]) & occupied[None, :]
    source = jnp.sum(jnp.where(place, ids[None, :], 0), axis=1)
    valid = jnp.where(ids < count, 1, 0)
    position = jnp.where(occupied, before, 0)
    return jnp.concatenate([send, source, valid, position, own_reads]).astype(jnp.int32)


def per_device(queries, keys, values, reads, grad_out):
    slots = 12
    tab = tables(reads, slots)
    q = queries.reshape(8, SEG, HQ * HD)
    g = grad_out.reshape(8, SEG, HQ * HD)
    whole = pl.BlockSpec(memory_space=pltpu.VMEM)
    unit = (ROWS, HD)
    out = pl.pallas_call(
        functools.partial(kernel, slots),
        out_shape=(
            jax.ShapeDtypeStruct(q.shape, BF16),
            jax.ShapeDtypeStruct(q.shape, BF16),
            jax.ShapeDtypeStruct((1, VT, 64), BF16),
            jax.ShapeDtypeStruct((1, VT, 64), BF16),
        ),
        in_specs=[pl.BlockSpec(memory_space=pltpu.SMEM)] + [whole] * 4,
        out_specs=(whole,) * 4,
        scratch_shapes=[pltpu.VMEM((KVH, 3, 4) + unit, BF16)] * 4
        + [pltpu.VMEM((KVH, 4, 4) + unit, BF16)] * 8
        + [pltpu.VMEM((KVH, JP, HD), BF16)] * 2
        + [pltpu.VMEM((KVH, HD, JP), BF16)] * 2
        + [pltpu.VMEM((16,) + unit, BF16)] * 2
        + [pltpu.VMEM((slots,) + unit, BF16)] * 2
        + [
            pltpu.VMEM((JP, 2 * ROWS), F32),
            pltpu.VMEM((JP, 2 * ROWS), BF16),
            pltpu.VMEM((JP, HD), F32),
            pltpu.VMEM((JP, HD), F32),
            pltpu.VMEM((KVH - 1, 2, VT16, HD), BF16),
            pltpu.VMEM((KVH - 1, 2, VT16, HD), BF16),
            pltpu.VMEM((2, VT16, HD), BF16),
            pltpu.VMEM((2, VT16, HD), BF16),
        ]
        + [pltpu.SemaphoreType.DMA((4, KVH, 3))] * 4
        + [pltpu.SemaphoreType.DMA((KVH - 1,))] * 2
        + [pltpu.SemaphoreType.DMA] * 2,
        compiler_params=pltpu.CompilerParams(
            collective_id=0, has_side_effects=True, vmem_limit_bytes=60 * 1024 * 1024
        ),
    )(tab, q, g, keys, values)
    attended, grad_queries, grad_keys, grad_values = out
    return (
        attended.reshape(queries.shape),
        grad_queries.reshape(queries.shape),
        grad_keys,
        grad_values,
    )


def solution(mesh):
    placed = (
        P(("seq", "enc"), None),
        P("enc", None, None),
        P("enc", None, None),
        P(),
        P(("seq", "enc"), None),
    )
    return jax.shard_map(
        per_device,
        mesh=mesh,
        in_specs=placed,
        out_specs=(
            P(("seq", "enc"), None),
            P(("seq", "enc"), None),
            P("enc", None, "seq"),
            P("enc", None, "seq"),
        ),
        check_vma=False,
    )
```

profile of v0, /device:TPU:32, one launch (start us, length us, event | category | flops | bytes accessed | tf_op | source)
XLA Modules:
  0.0 123.6 jit_solution(9126716875497245664)
XLA Ops:
  0.6 0.8 fusion.2
  1.4 0.9 dynamic-slice_reduce_fusion
  2.3 0.1 select_reduce_fusion.1
  2.4 0.1 select_reduce_fusion
  2.5 0.6 broadcast_select_fusion
  3.2 0.6 compare_select_fusion
  3.8 0.1 select_reduce_fusion.2
  3.9 0.6 concatenate.3.tab
  4.5 113.3 %shard_map.84 = (bf16[8,16,4096]{2,1,0:T(8,128)(2,1)}, bf16[8,16,4096]{2,1,0:T(8,128)(2,1)}, bf16[1,1601,64]{2,1,0:T(8,128)(2,1)}, bf16[1,1601,64]{2,1,0:T(8,128)(2,1)}) custom-call(s32[72]{0:T(128)} %concatenate.3.tab, bf16[8,16,4096]{2,1,0:T(8,128)(2,1)} %bitcast.6, bf16[8,16,4096]{2,1,0:T(8,128)(2,1)} %bitcast.7, bf16[1,1601,512]{2,1,0:T(8,128)(2,1)} %k_in.1, ...), custom_call_target="tpu_custom_call" | custom-call | tf_op jit(solution)/shard_map/pallas_call | solution.py:364
  117.8 0.0 copy-start.1
  117.8 0.0 copy-start
  117.8 2.0 %copy.11 = bf16[1,1601,64]{1,2,0:T(8,128)(2,1)} copy(bf16[1,1601,64]{2,1,0:T(8,128)(2,1)} %get-tuple-element.18) | data formatting | bytes 409856
  119.8 1.9 %copy.12 = bf16[1,1601,64]{1,2,0:T(8,128)(2,1)} copy(bf16[1,1601,64]{2,1,0:T(8,128)(2,1)} %get-tuple-element.19) | data formatting | bytes 409856
  121.7 0.0 copy-done.1
  121.7 1.0 copy.15
  122.6 0.0 copy-done
  122.7 1.0 copy.16
Async XLA Ops:
  117.8 3.9 %copy-start.1 = (bf16[8,16,4096]{2,1,0:T(8,128)(2,1)S(1)}, bf16[8,16,4096]{2,1,0:T(8,128)(2,1)}, u32[]{:S(2)}) copy-start(bf16[8,16,4096]{2,1,0:T(8,128)(2,1)} %get-tuple-element.8) | copy-start | bytes 3145732
  117.8 4.9 %copy-start = (bf16[8,16,4096]{2,1,0:T(8,128)(2,1)S(1)}, bf16[8,16,4096]{2,1,0:T(8,128)(2,1)}, u32[]{:S(2)}) copy-start(bf16[8,16,4096]{2,1,0:T(8,128)(2,1)} %get-tuple-element.9) | copy-start | bytes 3145732
where the time goes:
time: 125 us; the launch traced here: 124 us
  Pallas kernels  113 us (90%)
  local copies, waits for them, and re-layouts  7.3 us (6%)
  other arithmetic  2.38 us (2%)
    pallas_call x1, Pallas kernels, per_device(): pl.pallas_call(functools.partial(kernel, slots), out_shape=(jax.ShapeDtyp...  113 us
    unnamed x8, local copies, waits for them, and re-layouts  5.84 us

commit v1 on v0

v1 whole, which is shorter than its diff:
```python
import functools

import jax
import jax.numpy as jnp
from jax import lax
from jax.experimental import pallas as pl
from jax.experimental.pallas import tpu as pltpu
from jax.sharding import PartitionSpec as P

HQ = 32
KVH = 4
HD = 128
HALF = HQ // KVH // 2
SEG = 16
ROWS = HALF * SEG
STEPS = 2 * KVH
SLOTS = 12
WIDE = SLOTS * ROWS
VT = 1601
VT16 = 1616
JP = 1664
LOG2E = 1.4426950408889634
MESH = pl.DeviceIdType.MESH
BF16 = jnp.bfloat16
F32 = jnp.float32
CHUNKS = [(j, min(256, JP - j)) for j in range(0, JP, 256)]
NT = (((1,), (1,)), ((), ()))
IN, OUT = (0, 1), (2, 3)
AHEAD = 4
T_SEND, T_SRC, T_OK, T_POS = 0, 16, 32, 48


def kernel(
    reads, q_hbm, g_hbm, k_hbm, v_hbm, att_out, gq_out, gk_out, gv_out,
    tab, q_in, g_in, k_in, v_in, att_v, gq_v,
    a_q, a_g, a_o, a_d, m_q, m_g, m_o, m_d, r_q, r_g, r_o, r_d,
    kh, vh, kt, vt, stage_q, stage_g, pack_o, pack_d, s_scr, p_scr, k_acc, v_acc,
    z_send, z_recv, c_send, c_recv,
    s1, w1, s2, w2, zs, zw, cs, cw, ls, lo, lk,
):
    sq = lax.axis_index("seq")
    en = lax.axis_index("enc")
    z, core = sq // 2, sq % 2
    x, y = en // 4, en % 4
    scale = HD ** (-0.5)

    first = (a_q, a_g, a_o, a_d)
    middle = (m_q, m_g, m_o, m_d)
    last = (r_q, r_g, r_o, r_d)
    own = [(x, y), (y, x), (x, y), (y, x)]

    def peer(axis, d):
        if axis == 0:
            return (sq, ((x + d) % 4) * 4 + y)
        return (sq, x * 4 + (y + d) % 4)

    def hop1(ten, s, d):
        return pltpu.make_async_remote_copy(
            src_ref=first[ten].at[s, d - 1],
            dst_ref=middle[ten].at[s, :, own[ten][0]],
            send_sem=s1.at[ten, s, d - 1],
            recv_sem=w1.at[ten, s, d - 1],
            device_id=peer(ten % 2, d),
            device_id_type=MESH,
        )

    def hop2(ten, s, d):
        b = own[ten][1]
        return pltpu.make_async_remote_copy(
            src_ref=middle[ten].at[s, (b + d) % 4],
            dst_ref=last[ten].at[s, b],
            send_sem=s2.at[ten, s, d - 1],
            recv_sem=w2.at[ten, s, d - 1],
            device_id=peer(1 - ten % 2, d),
            device_id_type=MESH,
        )

    def start1(pair, s):
        for d in (2, 1, 3):
            for ten in pair:
                hop1(ten, s, d).start()

    def forward(pair, s):
        for ten in pair:
            for d in (1, 2, 3):
                hop1(ten, s, d).wait_recv()
            for d in (2, 1, 3):
                hop2(ten, s, d).start()

    def arrive(pair, s):
        for ten in pair:
            for d in (1, 2, 3):
                hop2(ten, s, d).wait_recv()

    def sent(pair, s):
        for ten in pair:
            for d in (1, 2, 3):
                hop1(ten, s, d).wait_send()
                hop2(ten, s, d).wait_send()

    def head_at(t):
        return (z + 1 + t) % 4

    def z_copy(t):
        return pltpu.make_async_remote_copy(
            src_ref=z_send.at[t],
            dst_ref=z_recv.at[t],
            send_sem=zs.at[t],
            recv_sem=zw.at[t],
            device_id=(head_at(t) * 2 + core, en),
            device_id_type=MESH,
        )

    def load(ten, t):
        cols = pl.ds(pl.multiple_of(head_at(t) * (2 * HALF * HD), 2 * HALF * HD), 2 * HALF * HD)
        src, dst = ((q_hbm, q_in), (g_hbm, g_in))[ten]
        return pltpu.make_async_copy(src.at[:, :, cols], dst.at[t], ls.at[ten, t])

    barrier = pltpu.get_barrier_semaphore()
    for d in (1, 2, 3):
        for target in (peer(0, d), peer(1, d), (((z + d) % 4) * 2 + core, en)):
            pl.semaphore_signal(barrier, inc=1, device_id=target, device_id_type=MESH)
    pl.semaphore_signal(barrier, inc=1, device_id=(z * 2 + 1 - core, en), device_id_type=MESH)
    for t in range(KVH):
        load(0, t).start()
        load(1, t).start()
    loads_kv = [
        pltpu.make_async_copy(k_hbm.at[0], k_in, lk.at[0]),
        pltpu.make_async_copy(v_hbm.at[0], v_in, lk.at[1]),
    ]
    for copy in loads_kv:
        copy.start()

    block_row = sq * 16 + en
    own_reads = [reads[r, block_row] for r in range(8)]
    for image in range(16):
        found = jnp.int32(0)
        for r in range(1, 8):
            found = jnp.where(own_reads[r] == image, r, found)
        tab[T_SEND + image] = found

    def pack_in(s):
        t, u = s // 2, s % 2
        cols = pl.ds(pl.multiple_of(u * (HALF * HD), HALF * HD), HALF * HD)
        for ten, src in ((0, q_in), (1, g_in)):
            a_own = own[ten][0]
            for d in range(4):
                a = (a_own + d) % 4
                for b in range(4):
                    image = a * 4 + b if ten == 0 else b * 4 + a
                    block = src[t, tab[T_SEND + image], :, cols]
                    for g in range(HALF):
                        piece = block[:, g * HD : (g + 1) * HD]
                        rows = pl.ds(g * SEG, SEG)
                        if d == 0:
                            middle[ten][s, b, a_own, rows, :] = piece
                        else:
                            first[ten][s, d - 1, b, rows, :] = piece

    for t in range(KVH):
        load(0, t).wait()
        load(1, t).wait()
    pack_in(jnp.int32(0))
    pl.semaphore_wait(barrier, 10)
    start1(IN, 0)

    def send_in(s, carry):
        pack_in(s)

        @pl.when(s < AHEAD)
        def _():
            start1(IN, s)

        return carry

    lax.fori_loop(1, STEPS, send_in, 0)

    count = jnp.int32(0)
    places = []
    for b in range(16):
        named = reads[0, sq * 16 + b] == en
        for r in range(1, 8):
            named = named | (reads[r, sq * 16 + b] == en)
        flag = jnp.where(named, 1, 0)
        tab[T_POS + b] = jnp.where(named, jnp.minimum(count, SLOTS - 1), 0)
        places.append(jnp.where(named, count, -1))
        count = count + flag
    for m in range(SLOTS):
        source = jnp.int32(0)
        for b in range(16):
            source = jnp.where(places[b] == m, b, source)
        tab[T_SRC + m] = source
        tab[T_OK + m] = jnp.where(count > m, 1, 0)

    forward(IN, 0)
    start1(IN, AHEAD)

    for copy in loads_kv:
        copy.wait()

    def heads(t, carry):
        cols = pl.ds(pl.multiple_of(head_at(t) * HD, HD), HD)
        for src, rows_ref, cols_ref in ((k_in, kh, kt), (v_in, vh, vt)):
            rows_ref[t, 0:1600, :] = src[0:1600, cols]
            tail = src[1600:VT, cols].astype(F32)
            mark = lax.broadcasted_iota(jnp.int32, (64, HD), 0) == 0
            rows_ref[t, 1600:JP, :] = jnp.where(
                mark, jnp.broadcast_to(tail, (64, HD)), 0.0
            ).astype(BF16)
            for j in range(0, JP, HD):
                cols_ref[t, :, j : j + HD] = rows_ref[t, j : j + HD, :].T
        return carry

    lax.fori_loop(0, 2, heads, 0)
    forward(IN, 1)
    start1(IN, AHEAD + 1)
    lax.fori_loop(2, KVH, heads, 0)
    forward(IN, 2)
    start1(IN, AHEAD + 2)

    def step(s, carry):
        t, u = s // 2, s % 2
        arrive(IN, s)
        for ten, stage in ((0, stage_q), (1, stage_g)):
            b_own = own[ten][1]
            for d in range(4):
                b = (b_own + d) % 4
                for a in range(4):
                    if d == 0:
                        stage[b * 4 + a] = middle[ten][s, b, a]
                    else:
                        stage[b * 4 + a] = last[ten][s, b, a]

        @pl.when(s + 3 < STEPS)
        def _():
            forward(IN, s + 3)

        @pl.when(s + 3 + AHEAD < STEPS)
        def _():
            start1(IN, s + 3 + AHEAD)

        @pl.when(u == 0)
        def _():
            k_acc[...] = jnp.zeros_like(k_acc)
            v_acc[...] = jnp.zeros_like(v_acc)

        q_parts, g_parts = [], []
        for m in range(SLOTS):
            source = tab[T_SRC + m]
            q_parts.append(stage_q[(source % 4) * 4 + source // 4])
            g_parts.append(jnp.where(tab[T_OK + m] > 0, stage_g[source].astype(F32), 0.0))
        q = jnp.concatenate(q_parts, axis=0)
        g_t = jnp.concatenate(g_parts, axis=0).T

        top = jnp.full((8, WIDE), -jnp.inf, F32)
        for j, n in CHUNKS:
            sc = lax.dot_general(kh[t, j : j + n, :], q, NT, preferred_element_type=F32)
            if j + n > VT:
                row = lax.broadcasted_iota(jnp.int32, sc.shape, 0) + j
                sc = jnp.where(row < VT, sc, -1e30)
            s_scr[j : j + n, :] = sc
            top = jnp.maximum(top, jnp.max(sc.reshape(n // 8, 8, WIDE), axis=0))
        c2 = scale * LOG2E
        top2 = jnp.max(top, axis=0, keepdims=True) * c2
        total = jnp.zeros((8, WIDE), F32)
        o_t = jnp.zeros((HD, WIDE), F32)
        for j, n in CHUNKS:
            p = jnp.exp2(s_scr[j : j + n, :] * c2 - top2)
            total += jnp.sum(p.reshape(n // 8, 8, WIDE), axis=0)
            p_b = p.astype(BF16)
            p_scr[j : j + n, :] = p_b
            o_t += jnp.dot(vt[t, :, j : j + n], p_b, preferred_element_type=F32)
        inv = 1.0 / jnp.sum(total, axis=0, keepdims=True)
        o_t = (o_t * inv).astype(BF16).astype(F32)
        pack_o[...] = o_t.T.astype(BF16).reshape(SLOTS, ROWS, HD)

        @pl.when(s > 1)
        def _():
            forward(OUT, s - 2)

        delta = jnp.sum(g_t * o_t, axis=0, keepdims=True) * inv
        g_s = (g_t * inv).astype(BF16)
        d_t = jnp.zeros((HD, WIDE), F32)
        for j, n in CHUNKS:
            dp = jnp.dot(vh[t, j : j + n, :], g_s, preferred_element_type=F32)
            p_b = p_scr[j : j + n, :]
            ds = (p_b.astype(F32) * (dp - delta)).astype(BF16)
            v_acc[j : j + n, :] += lax.dot_general(p_b, g_s, NT, preferred_element_type=F32)
            k_acc[j : j + n, :] += jnp.dot(ds, q, preferred_element_type=F32)
            d_t += jnp.dot(kt[t, :, j : j + n], ds, preferred_element_type=F32)
        pack_d[...] = (d_t * scale).T.astype(BF16).reshape(SLOTS, ROWS, HD)

        for ten, packed in ((2, pack_o), (3, pack_d)):
            a_own = own[ten][0]
            for d in range(4):
                a = (a_own + d) % 4
                for b in range(4):
                    block = a * 4 + b if ten == 2 else b * 4 + a
                    piece = packed[tab[T_POS + block]]
                    if d == 0:
                        middle[ten][s, b, a_own] = piece
                    else:
                        first[ten][s, d - 1, b] = piece
        start1(OUT, s)

        @pl.when((u == 1) & (t < KVH - 1))
        def _():
            z_send[t, 0] = (k_acc[0:VT16, :] * scale).astype(BF16)
            z_send[t, 1] = v_acc[0:VT16, :].astype(BF16)
            z_copy(t).start()

        return carry

    lax.fori_loop(0, STEPS, step, 0)

    parts = [(j, min(256, VT16 - j)) for j in range(0, VT16, 256)]
    for t in range(KVH - 1):
        z_copy(t).wait_recv()
    forward(OUT, STEPS - 2)
    for j, n in parts:
        rows = pl.ds(j, n)
        sums = [k_acc[rows, :] * scale, v_acc[rows, :]]
        for w, acc in ((0, k_acc), (1, v_acc)):
            for t in range(KVH - 1):
                sums[w] = sums[w] + z_recv[t, w, rows, :].astype(F32)
            acc[rows, :] = sums[w]
            c_send[w, rows, :] = sums[w].astype(BF16)
    core_copy = pltpu.make_async_remote_copy(
        src_ref=c_send,
        dst_ref=c_recv,
        send_sem=cs,
        recv_sem=cw,
        device_id=(z * 2 + 1 - core, en),
        device_id_type=MESH,
    )
    core_copy.start()
    forward(OUT, STEPS - 1)

    def out_copy(ten, s):
        cols = pl.ds(
            pl.multiple_of((head_at(s // 2) * 2 + s % 2) * (HALF * HD), HALF * HD), HALF * HD
        )
        src, dst = ((att_v, att_out), (gq_v, gq_out))[ten - 2]
        return pltpu.make_async_copy(src.at[s], dst.at[:, :, cols], lo.at[ten - 2, s])

    def collect(s, carry):
        arrive(OUT, s)
        for ten, stage, out in ((2, stage_q, att_v), (3, stage_g, gq_v)):
            b_own = own[ten][1]
            for d in range(4):
                b = (b_own + d) % 4
                for a in range(4):
                    src = middle[ten] if d == 0 else last[ten]
                    stage[b * 4 + a] = src[s, b, a]
            for r in range(8):
                image = reads[r, block_row]
                if ten == 2:
                    block = stage[(image % 4) * 4 + image // 4]
                else:
                    block = stage[image]
                for g in range(HALF):
                    out[s, r, :, g * HD : (g + 1) * HD] = block[g * SEG : (g + 1) * SEG, :]
            out_copy(ten, s).start()
        return carry

    def finish(s, carry):
        sent(IN, s)
        sent(OUT, s)
        out_copy(2, s).wait()
        out_copy(3, s).wait()
        return carry

    lax.fori_loop(0, STEPS - 2, collect, 0)
    core_copy.wait_recv()
    for w, acc, out in ((0, k_acc, gk_out), (1, v_acc, gv_out)):
        for j in range(0, VT, HD):
            n = min(HD, VT16 - j)
            full = acc[j : j + n, :] + c_recv[w, j : j + n, :].astype(F32)
            if n < HD:
                full = jnp.concatenate([full, jnp.zeros((HD - n, HD), F32)], axis=0)
            turned = full.T
            half = jnp.where(core == 0, turned[0:64], turned[64:128]).astype(BF16)
            if j + HD > VT:
                out[0, :, j:VT] = half[:, 0 : VT - j]
            else:
                out[0, :, j : j + HD] = half
    lax.fori_loop(0, STEPS - 2, finish, 0)
    for t in range(KVH - 1):
        z_copy(t).wait_send()
    core_copy.wait_send()
    lax.fori_loop(STEPS - 2, STEPS, collect, 0)
    lax.fori_loop(STEPS - 2, STEPS, finish, 0)


def per_device(queries, keys, values, reads, grad_out):
    q = queries.reshape(8, SEG, HQ * HD)
    g = grad_out.reshape(8, SEG, HQ * HD)
    vmem = pl.BlockSpec(memory_space=pltpu.VMEM)
    hbm = pl.BlockSpec(memory_space=pl.ANY)
    unit = (ROWS, HD)
    attended, grad_queries, grad_keys, grad_values = pl.pallas_call(
        kernel,
        out_shape=(
            jax.ShapeDtypeStruct(q.shape, BF16),
            jax.ShapeDtypeStruct(q.shape, BF16),
            jax.ShapeDtypeStruct((1, 64, VT), BF16),
            jax.ShapeDtypeStruct((1, 64, VT), BF16),
        ),
        in_specs=[pl.BlockSpec(memory_space=pltpu.SMEM)] + [hbm] * 4,
        out_specs=(hbm, hbm, vmem, vmem),
        scratch_shapes=[pltpu.SMEM((64,), jnp.int32)]
        + [pltpu.VMEM((KVH, 8, SEG, 2 * HALF * HD), BF16)] * 2
        + [pltpu.VMEM((VT, KVH * HD), BF16)] * 2
        + [pltpu.VMEM((STEPS, 8, SEG, HALF * HD), BF16)] * 2
        + [pltpu.VMEM((STEPS, 3, 4) + unit, BF16)] * 4
        + [pltpu.VMEM((STEPS, 4, 4) + unit, BF16)] * 8
        + [pltpu.VMEM((KVH, JP, HD), BF16)] * 2
        + [pltpu.VMEM((KVH, HD, JP), BF16)] * 2
        + [pltpu.VMEM((16,) + unit, BF16)] * 2
        + [pltpu.VMEM((SLOTS,) + unit, BF16)] * 2
        + [
            pltpu.VMEM((JP, WIDE), F32),
            pltpu.VMEM((JP, WIDE), BF16),
            pltpu.VMEM((JP, HD), F32),
            pltpu.VMEM((JP, HD), F32),
            pltpu.VMEM((KVH - 1, 2, VT16, HD), BF16),
            pltpu.VMEM((KVH - 1, 2, VT16, HD), BF16),
            pltpu.VMEM((2, VT16, HD), BF16),
            pltpu.VMEM((2, VT16, HD), BF16),
        ]
        + [pltpu.SemaphoreType.DMA((4, STEPS, 3))] * 4
        + [pltpu.SemaphoreType.DMA((KVH - 1,))] * 2
        + [pltpu.SemaphoreType.DMA] * 2
        + [
            pltpu.SemaphoreType.DMA((2, KVH)),
            pltpu.SemaphoreType.DMA((2, STEPS)),
            pltpu.SemaphoreType.DMA((2,)),
        ],
        compiler_params=pltpu.CompilerParams(
            collective_id=0, has_side_effects=True, vmem_limit_bytes=62 * 1024 * 1024
        ),
    )(reads.T, q, g, keys, values)
    return (
        attended.reshape(queries.shape),
        grad_queries.reshape(queries.shape),
        jnp.swapaxes(grad_keys, 1, 2),
        jnp.swapaxes(grad_values, 1, 2),
    )


def solution(mesh):
    placed = (
        P(("seq", "enc"), None),
        P("enc", None, None),
        P("enc", None, None),
        P(),
        P(("seq", "enc"), None),
    )
    return jax.shard_map(
        per_device,
        mesh=mesh,
        in_specs=placed,
        out_specs=(
            P(("seq", "enc"), None),
            P(("seq", "enc"), None),
            P("enc", None, "seq"),
            P("enc", None, "seq"),
        ),
        check_vma=False,
    )
```

time: 125 us -> 111 us (0.89); the launches traced: 124 us -> 111 us
  Pallas kernels: 113 us -> 106 us
  local copies, waits for them, and re-layouts: 7.3 us -> 4.73 us
  other arithmetic: 2.38 us -> 0 us
    pallas_call x1, Pallas kernels: 113 us -> 106 us  [per_device(): pl.pallas_call(kernel, out_shape=(jax.ShapeDtypeStruct(q.shape, BF16), ja...]
    select_n x2 -> x0, other arithmetic: 1.29 us -> none  [the longest x1 0.65 us: tables(): valid = jnp.where(ids < count, 1, 0)]
    unnamed x8 -> x10, local copies, waits for them, and re-layouts: 5.84 us -> 4.73 us
where the time goes in v1:
time: 111 us
  Pallas kernels  106 us (95%)
  local copies, waits for them, and re-layouts  4.73 us (4%)
    pallas_call x1, Pallas kernels, per_device(): pl.pallas_call(kernel, out_shape=(jax.ShapeDtypeStruct(q.shape, BF16), ja...  106 us
    unnamed x10, local copies, waits for them, and re-layouts  4.73 us

profile of v1, /device:TPU:32, one launch (start us, length us, event | category | flops | bytes accessed | tf_op | source)
XLA Modules:
  0.0 111.2 jit_solution(16397388862064771959)
XLA Ops:
  0.6 105.8 %shard_map.84 = (bf16[8,16,4096]{2,1,0:T(8,128)(2,1)}, bf16[8,16,4096]{2,1,0:T(8,128)(2,1)}, bf16[1,64,1601]{2,1,0:T(8,128)(2,1)}, bf16[1,64,1601]{2,1,0:T(8,128)(2,1)}) custom-call(s32[8,128]{1,0:T(8,128)} %bitcast.13, bf16[8,16,4096]{2,1,0:T(8,128)(2,1)} %bitcast.9, bf16[8,16,4096]{2,1,0:T(8,128)(2,1)} %bitcast.10, bf16[1,1601,512]{2,1,0:T(8,128)(2,1)} %k_hbm.1, ...), custom_call_target="tpu_custom_call" | custom-call | tf_op jit(solution)/shard_map/pallas_call | solution.py:401
  106.4 0.0 copy-start
  106.4 0.0 copy-start.2
  106.5 2.4 %copy.13 = bf16[128,4096]{1,0:T(8,128)(2,1)} copy(bf16[128,4096]{1,0:T(8,128)(2,1)} %bitcast.8) | data formatting | bytes 2097152
  108.8 0.0 copy-done
  108.8 0.0 copy-start.1
  108.8 1.0 copy.14
  109.8 0.0 copy-done.2
  109.8 0.7 copy.15
  110.5 0.0 copy-done.1
  110.5 0.7 copy.16
Async XLA Ops:
  106.4 2.4 %copy-start = (bf16[8,16,4096]{2,1,0:T(8,128)(2,1)S(1)}, bf16[8,16,4096]{2,1,0:T(8,128)(2,1)}, u32[]{:S(2)}) copy-start(bf16[8,16,4096]{2,1,0:T(8,128)(2,1)} %get-tuple-element.9) | copy-start | bytes 3145732
  106.4 3.4 %copy-start.2 = (bf16[1,64,1601]{2,1,0:T(8,128)(2,1)S(1)}, bf16[1,64,1601]{2,1,0:T(8,128)(2,1)}, u32[]{:S(2)}) copy-start(bf16[1,64,1601]{2,1,0:T(8,128)(2,1)} %get-tuple-element.10) | copy-start | bytes 614788
  108.8 1.7 %copy-start.1 = (bf16[1,64,1601]{2,1,0:T(8,128)(2,1)S(1)}, bf16[1,64,1601]{2,1,0:T(8,128)(2,1)}, u32[]{:S(2)}) copy-start(bf16[1,64,1601]{2,1,0:T(8,128)(2,1)} %get-tuple-element.11) | copy-start | bytes 614788

commit v2 on v1

--- a/solution.py
+++ b/solution.py
@@ -32,11 +32,11 @@
 
 def kernel(
     reads, q_hbm, g_hbm, k_hbm, v_hbm, att_out, gq_out, gk_out, gv_out,
-    tab, q_in, g_in, k_in, v_in, att_v, gq_v,
+    tab, q_0, g_0, q_in, g_in, k_in, v_in, att_v, gq_v,
     a_q, a_g, a_o, a_d, m_q, m_g, m_o, m_d, r_q, r_g, r_o, r_d,
     kh, vh, kt, vt, stage_q, stage_g, pack_o, pack_d, s_scr, p_scr, k_acc, v_acc,
     z_send, z_recv, c_send, c_recv,
-    s1, w1, s2, w2, zs, zw, cs, cw, ls, lo, lk,
+    s1, w1, s2, w2, zs, zw, cs, cw, l0, ls, lo, lk,
 ):
     sq = lax.axis_index("seq")
     en = lax.axis_index("enc")
@@ -58,8 +58,8 @@
         return pltpu.make_async_remote_copy(
             src_ref=first[ten].at[s, d - 1],
             dst_ref=middle[ten].at[s, :, own[ten][0]],
-            send_sem=s1.at[ten, s, d - 1],
-            recv_sem=w1.at[ten, s, d - 1],
+            send_sem=s1.at[ten],
+            recv_sem=w1.at[ten, s],
             device_id=peer(ten % 2, d),
             device_id_type=MESH,
         )
@@ -69,8 +69,8 @@
         return pltpu.make_async_remote_copy(
             src_ref=middle[ten].at[s, (b + d) % 4],
             dst_ref=last[ten].at[s, b],
-            send_sem=s2.at[ten, s, d - 1],
-            recv_sem=w2.at[ten, s, d - 1],
+            send_sem=s2.at[ten],
+            recv_sem=w2.at[ten // 2, s],
             device_id=peer(1 - ten % 2, d),
             device_id_type=MESH,
         )
@@ -80,23 +80,26 @@
             for ten in pair:
                 hop1(ten, s, d).start()
 
+    def await_recv(ref, sem):
+        pltpu.make_async_remote_copy(
+            src_ref=ref, dst_ref=ref, send_sem=s1.at[0], recv_sem=sem,
+            device_id=peer(0, 1), device_id_type=MESH,
+        ).wait_recv()
+
+    def await_send(ref, sem):
+        pltpu.make_async_remote_copy(
+            src_ref=ref, dst_ref=ref, send_sem=sem, recv_sem=w1.at[0, 0],
+            device_id=peer(0, 1), device_id_type=MESH,
+        ).wait_send()
+
     def forward(pair, s):
         for ten in pair:
-            for d in (1, 2, 3):
-                hop1(ten, s, d).wait_recv()
+            await_recv(first[ten].at[s], w1.at[ten, s])
             for d in (2, 1, 3):
                 hop2(ten, s, d).start()
 
     def arrive(pair, s):
-        for ten in pair:
-            for d in (1, 2, 3):
-                hop2(ten, s, d).wait_recv()
-
-    def sent(pair, s):
-        for ten in pair:
-            for d in (1, 2, 3):
-                hop1(ten, s, d).wait_send()
-                hop2(ten, s, d).wait_send()
+        await_recv(first[pair[0]].at[pl.ds(0, 2)], w2.at[pair[0] // 2, s])
 
     def head_at(t):
         return (z + 1 + t) % 4
@@ -114,7 +117,9 @@
     def load(ten, t):
         cols = pl.ds(pl.multiple_of(head_at(t) * (2 * HALF * HD), 2 * HALF * HD), 2 * HALF * HD)
         src, dst = ((q_hbm, q_in), (g_hbm, g_in))[ten]
-        return pltpu.make_async_copy(src.at[:, :, cols], dst.at[t], ls.at[ten, t])
+        if t == 0:
+            return pltpu.make_async_copy(src.at[:, :, cols], (q_0, g_0)[ten], l0.at[ten])
+        return pltpu.make_async_copy(src.at[:, :, cols], dst.at[t - 1], ls.at[ten])
 
     barrier = pltpu.get_barrier_semaphore()
     for d in (1, 2, 3):
@@ -139,16 +144,15 @@
             found = jnp.where(own_reads[r] == image, r, found)
         tab[T_SEND + image] = found
 
-    def pack_in(s):
-        t, u = s // 2, s % 2
+    def pack_in(s, u, sources):
         cols = pl.ds(pl.multiple_of(u * (HALF * HD), HALF * HD), HALF * HD)
-        for ten, src in ((0, q_in), (1, g_in)):
+        for ten, src in ((0, sources[0]), (1, sources[1])):
             a_own = own[ten][0]
             for d in range(4):
                 a = (a_own + d) % 4
                 for b in range(4):
                     image = a * 4 + b if ten == 0 else b * 4 + a
-                    block = src[t, tab[T_SEND + image], :, cols]
+                    block = src[tab[T_SEND + image], :, cols]
                     for g in range(HALF):
                         piece = block[:, g * HD : (g + 1) * HD]
                         rows = pl.ds(g * SEG, SEG)
@@ -157,15 +161,18 @@
                         else:
                             first[ten][s, d - 1, b, rows, :] = piece
 
-    for t in range(KVH):
-        load(0, t).wait()
-        load(1, t).wait()
-    pack_in(jnp.int32(0))
+    load(0, 0).wait()
+    load(1, 0).wait()
+    pack_in(0, 0, (q_0, g_0))
     pl.semaphore_wait(barrier, 10)
     start1(IN, 0)
+    pack_in(1, 1, (q_0, g_0))
+    start1(IN, 1)
+    pltpu.make_async_copy(q_in, q_in, ls.at[0]).wait()
+    pltpu.make_async_copy(g_in, g_in, ls.at[1]).wait()
 
     def send_in(s, carry):
-        pack_in(s)
+        pack_in(s, s % 2, (q_in.at[s // 2 - 1], g_in.at[s // 2 - 1]))
 
         @pl.when(s < AHEAD)
         def _():
@@ -173,7 +180,7 @@
 
         return carry
 
-    lax.fori_loop(1, STEPS, send_in, 0)
+    lax.fori_loop(2, STEPS, send_in, 0)
 
     count = jnp.int32(0)
     places = []
@@ -341,7 +348,7 @@
             pl.multiple_of((head_at(s // 2) * 2 + s % 2) * (HALF * HD), HALF * HD), HALF * HD
         )
         src, dst = ((att_v, att_out), (gq_v, gq_out))[ten - 2]
-        return pltpu.make_async_copy(src.at[s], dst.at[:, :, cols], lo.at[ten - 2, s])
+        return pltpu.make_async_copy(src.at[s], dst.at[:, :, cols], lo.at[ten - 2])
 
     def collect(s, carry):
         arrive(OUT, s)
@@ -363,13 +370,6 @@
             out_copy(ten, s).start()
         return carry
 
-    def finish(s, carry):
-        sent(IN, s)
-        sent(OUT, s)
-        out_copy(2, s).wait()
-        out_copy(3, s).wait()
-        return carry
-
     lax.fori_loop(0, STEPS - 2, collect, 0)
     core_copy.wait_recv()
     for w, acc, out in ((0, k_acc, gk_out), (1, v_acc, gv_out)):
@@ -384,12 +384,36 @@
                 out[0, :, j:VT] = half[:, 0 : VT - j]
             else:
                 out[0, :, j : j + HD] = half
-    lax.fori_loop(0, STEPS - 2, finish, 0)
     for t in range(KVH - 1):
         z_copy(t).wait_send()
     core_copy.wait_send()
     lax.fori_loop(STEPS - 2, STEPS, collect, 0)
-    lax.fori_loop(STEPS - 2, STEPS, finish, 0)
+    for ten in range(4):
+        await_send(first[ten], s1.at[ten])
+        await_send(first[ten], s2.at[ten])
+    pltpu.make_async_copy(att_v, att_v, lo.at[0]).wait()
+    pltpu.make_async_copy(gq_v, gq_v, lo.at[1]).wait()
+
+
+def copy_out(*refs):
+    sources, targets, buffers, sems = refs[0:4], refs[4:8], refs[8:12], refs[12]
+    copies = []
+    for i in range(4):
+        rows = sources[i].shape[0]
+        for p in range(2 if rows > 1 else 1):
+            part = pl.ds(p * (rows // 2), rows // 2) if rows > 1 else pl.ds(0, 1)
+            into = pltpu.make_async_copy(
+                sources[i].at[part], buffers[i].at[part], sems.at[0, i, p]
+            )
+            into.start()
+            copies.append(
+                (into, pltpu.make_async_copy(buffers[i].at[part], targets[i].at[part], sems.at[1, i, p]))
+            )
+    for into, back in copies:
+        into.wait()
+        back.start()
+    for into, back in copies:
+        back.wait()
 
 
 def per_device(queries, keys, values, reads, grad_out):
@@ -398,7 +422,7 @@
     vmem = pl.BlockSpec(memory_space=pltpu.VMEM)
     hbm = pl.BlockSpec(memory_space=pl.ANY)
     unit = (ROWS, HD)
-    attended, grad_queries, grad_keys, grad_values = pl.pallas_call(
+    results = pl.pallas_call(
         kernel,
         out_shape=(
             jax.ShapeDtypeStruct(q.shape, BF16),
@@ -409,7 +433,8 @@
         in_specs=[pl.BlockSpec(memory_space=pltpu.SMEM)] + [hbm] * 4,
         out_specs=(hbm, hbm, vmem, vmem),
         scratch_shapes=[pltpu.SMEM((64,), jnp.int32)]
-        + [pltpu.VMEM((KVH, 8, SEG, 2 * HALF * HD), BF16)] * 2
+        + [pltpu.VMEM((8, SEG, 2 * HALF * HD), BF16)] * 2
+        + [pltpu.VMEM((KVH - 1, 8, SEG, 2 * HALF * HD), BF16)] * 2
         + [pltpu.VMEM((VT, KVH * HD), BF16)] * 2
         + [pltpu.VMEM((STEPS, 8, SEG, HALF * HD), BF16)] * 2
         + [pltpu.VMEM((STEPS, 3, 4) + unit, BF16)] * 4
@@ -428,18 +453,32 @@
             pltpu.VMEM((2, VT16, HD), BF16),
             pltpu.VMEM((2, VT16, HD), BF16),
         ]
-        + [pltpu.SemaphoreType.DMA((4, STEPS, 3))] * 4
+        + [
+            pltpu.SemaphoreType.DMA((4,)),
+            pltpu.SemaphoreType.DMA((4, STEPS)),
+            pltpu.SemaphoreType.DMA((4,)),
+            pltpu.SemaphoreType.DMA((2, STEPS)),
+        ]
         + [pltpu.SemaphoreType.DMA((KVH - 1,))] * 2
         + [pltpu.SemaphoreType.DMA] * 2
         + [
-            pltpu.SemaphoreType.DMA((2, KVH)),
-            pltpu.SemaphoreType.DMA((2, STEPS)),
+            pltpu.SemaphoreType.DMA((2,)),
+            pltpu.SemaphoreType.DMA((2,)),
+            pltpu.SemaphoreType.DMA((2,)),
             pltpu.SemaphoreType.DMA((2,)),
         ],
         compiler_params=pltpu.CompilerParams(
             collective_id=0, has_side_effects=True, vmem_limit_bytes=62 * 1024 * 1024
         ),
     )(reads.T, q, g, keys, values)
+    attended, grad_queries, grad_keys, grad_values = pl.pallas_call(
+        copy_out,
+        out_shape=tuple(jax.ShapeDtypeStruct(r.shape, r.dtype) for r in results),
+        in_specs=[hbm] * 4,
+        out_specs=(hbm,) * 4,
+        scratch_shapes=[pltpu.VMEM(r.shape, r.dtype) for r in results]
+        + [pltpu.SemaphoreType.DMA((2, 4, 2))],
+    )(*results)
     return (
         attended.reshape(queries.shape),
         grad_queries.reshape(queries.shape),

time: 111 us -> 106 us (0.955)
  local copies, waits for them, and re-layouts: 4.73 us -> 0 us
    unnamed x10 -> x0, local copies, waits for them, and re-layouts: 4.73 us -> none
    pallas_call x1, Pallas kernels: 106 us -> 102 us  [per_device(): pl.pallas_call(kernel, out_shape=(jax.ShapeDtypeStruct(q.shape, BF16), ja...]
    pallas_call x0 -> x1, Pallas kernels: none -> 2.63 us  [per_device(): pl.pallas_call(copy_out, out_shape=tuple((jax.ShapeDtypeStruct(r.shape, r...]
where the time goes in v2:
time: 106 us; the launch traced here: 105 us
  Pallas kernels  105 us (99%)
    pallas_call x1, Pallas kernels, per_device(): pl.pallas_call(kernel, out_shape=(jax.ShapeDtypeStruct(q.shape, BF16), ja...  102 us
    pallas_call x1, Pallas kernels, per_device(): pl.pallas_call(copy_out, out_shape=tuple((jax.ShapeDtypeStruct(r.shape, r...  2.63 us

profile of v2, /device:TPU:32, one launch (start us, length us, event | category | flops | bytes accessed | tf_op | source)
XLA Modules:
  0.0 105.4 jit_solution(17133847950227722286)
XLA Ops:
  0.6 102.2 %shard_map.84 = (bf16[8,16,4096]{2,1,0:T(8,128)(2,1)}, bf16[8,16,4096]{2,1,0:T(8,128)(2,1)}, bf16[1,64,1601]{2,1,0:T(8,128)(2,1)}, bf16[1,64,1601]{2,1,0:T(8,128)(2,1)}) custom-call(s32[8,128]{1,0:T(8,128)} %bitcast.9, bf16[8,16,4096]{2,1,0:T(8,128)(2,1)} %bitcast.7, bf16[8,16,4096]{2,1,0:T(8,128)(2,1)} %bitcast.8, bf16[1,1601,512]{2,1,0:T(8,128)(2,1)} %k_hbm.1, ...), custom_call_target="tpu_custom_call" | custom-call | tf_op jit(solution)/shard_map/pallas_call | solution.py:425
  102.8 2.6 %shard_map.85 = (bf16[8,16,4096]{2,1,0:T(8,128)(2,1)}, bf16[8,16,4096]{2,1,0:T(8,128)(2,1)}, bf16[1,64,1601]{2,1,0:T(8,128)(2,1)}, bf16[1,64,1601]{2,1,0:T(8,128)(2,1)}) custom-call(bf16[8,16,4096]{2,1,0:T(8,128)(2,1)} %get-tuple-element.12.refs_0_, bf16[8,16,4096]{2,1,0:T(8,128)(2,1)} %get-tuple-element.13.refs_1_, ...), custom_call_target="tpu_custom_call" | custom-call | tf_op jit(solution)/shard_map/pallas_call | solution.py:474

commit v3 on v2

--- a/solution.py
+++ b/solution.py
@@ -31,12 +31,12 @@
 
 
 def kernel(
-    reads, q_hbm, g_hbm, k_hbm, v_hbm, att_out, gq_out, gk_out, gv_out,
-    tab, q_0, g_0, q_in, g_in, k_in, v_in, att_v, gq_v,
+    reads_hbm, q_hbm, g_hbm, k_hbm, v_hbm, att_out, gq_out, gk_out, gv_out, end_o, end_d,
+    reads, tab, q_0, g_0, q_in, g_in, k_in, v_in, att_v, gq_v, gk_v, gv_v,
     a_q, a_g, a_o, a_d, m_q, m_g, m_o, m_d, r_q, r_g, r_o, r_d,
     kh, vh, kt, vt, stage_q, stage_g, pack_o, pack_d, s_scr, p_scr, k_acc, v_acc,
     z_send, z_recv, c_send, c_recv,
-    s1, w1, s2, w2, zs, zw, cs, cw, l0, ls, lo, lk,
+    s1, w1, s2, w2, zs, zw, cs, cw, l0, ls, lo, lk, le, lr,
 ):
     sq = lax.axis_index("seq")
     en = lax.axis_index("enc")
@@ -66,9 +66,10 @@
 
     def hop2(ten, s, d):
         b = own[ten][1]
+        final = ten in OUT and isinstance(s, int) and s == STEPS - 1
         return pltpu.make_async_remote_copy(
             src_ref=middle[ten].at[s, (b + d) % 4],
-            dst_ref=last[ten].at[s, b],
+            dst_ref=(end_o, end_d)[ten - 2].at[b] if final else last[ten].at[s, b],
             send_sem=s2.at[ten],
             recv_sem=w2.at[ten // 2, s],
             device_id=peer(1 - ten % 2, d),
@@ -126,6 +127,8 @@
         for target in (peer(0, d), peer(1, d), (((z + d) % 4) * 2 + core, en)):
             pl.semaphore_signal(barrier, inc=1, device_id=target, device_id_type=MESH)
     pl.semaphore_signal(barrier, inc=1, device_id=(z * 2 + 1 - core, en), device_id_type=MESH)
+    table = pltpu.make_async_copy(reads_hbm, reads, lr)
+    table.start()
     for t in range(KVH):
         load(0, t).start()
         load(1, t).start()
@@ -137,6 +140,7 @@
         copy.start()
 
     block_row = sq * 16 + en
+    table.wait()
     own_reads = [reads[r, block_row] for r in range(8)]
     for image in range(16):
         found = jnp.int32(0)
@@ -342,6 +346,16 @@
     )
     core_copy.start()
     forward(OUT, STEPS - 1)
+    ends = []
+    for ten, end in ((2, end_o), (3, end_d)):
+        b_own = own[ten][1]
+        ends.append(
+            pltpu.make_async_copy(
+                middle[ten].at[STEPS - 1, b_own], end.at[b_own], le.at[ten - 2]
+            )
+        )
+    for copy in ends:
+        copy.start()
 
     def out_copy(ten, s):
         cols = pl.ds(
@@ -370,9 +384,9 @@
             out_copy(ten, s).start()
         return carry
 
-    lax.fori_loop(0, STEPS - 2, collect, 0)
+    lax.fori_loop(0, STEPS - 3, collect, 0)
     core_copy.wait_recv()
-    for w, acc, out in ((0, k_acc, gk_out), (1, v_acc, gv_out)):
+    for w, acc, out in ((0, k_acc, gk_v), (1, v_acc, gv_v)):
         for j in range(0, VT, HD):
             n = min(HD, VT16 - j)
             full = acc[j : j + n, :] + c_recv[w, j : j + n, :].astype(F32)
@@ -384,42 +398,82 @@
                 out[0, :, j:VT] = half[:, 0 : VT - j]
             else:
                 out[0, :, j : j + HD] = half
+    gradients = [
+        pltpu.make_async_copy(gk_v, gk_out, le.at[2]),
+        pltpu.make_async_copy(gv_v, gv_out, le.at[3]),
+    ]
+    for copy in gradients:
+        copy.start()
     for t in range(KVH - 1):
         z_copy(t).wait_send()
     core_copy.wait_send()
-    lax.fori_loop(STEPS - 2, STEPS, collect, 0)
+    lax.fori_loop(STEPS - 3, STEPS - 1, collect, 0)
     for ten in range(4):
         await_send(first[ten], s1.at[ten])
-        await_send(first[ten], s2.at[ten])
+        if ten in IN:
+            await_send(first[ten], s2.at[ten])
     pltpu.make_async_copy(att_v, att_v, lo.at[0]).wait()
     pltpu.make_async_copy(gq_v, gq_v, lo.at[1]).wait()
-
-
-def copy_out(*refs):
-    sources, targets, buffers, sems = refs[0:4], refs[4:8], refs[8:12], refs[12]
-    copies = []
-    for i in range(4):
-        rows = sources[i].shape[0]
-        for p in range(2 if rows > 1 else 1):
-            part = pl.ds(p * (rows // 2), rows // 2) if rows > 1 else pl.ds(0, 1)
-            into = pltpu.make_async_copy(
-                sources[i].at[part], buffers[i].at[part], sems.at[0, i, p]
-            )
-            into.start()
-            copies.append(
-                (into, pltpu.make_async_copy(buffers[i].at[part], targets[i].at[part], sems.at[1, i, p]))
-            )
-    for into, back in copies:
-        into.wait()
-        back.start()
-    for into, back in copies:
-        back.wait()
+    for copy in ends + gradients:
+        copy.wait()
+    for ten in OUT:
+        await_send(first[ten], s2.at[ten])
+    arrive(OUT, STEPS - 1)
+
+
+def copy_out(reads_hbm, att, gq, gk, gv, end_o, end_d, att_out, gq_out, gk_out, gv_out,
+             reads, att_v, gq_v, gk_v, gv_v, end_ov, end_dv, into_sem, back_sem):
+    sq = lax.axis_index("seq")
+    en = lax.axis_index("enc")
+    block_row = sq * 16 + en
+    cols0 = ((sq // 2) * 2 + 1) * (HALF * HD)
+
+    def into(src, dst, i):
+        copy = pltpu.make_async_copy(src, dst, into_sem.at[i])
+        copy.start()
+        return copy
+
+    ends = [into(reads_hbm, reads, 8), into(end_o, end_ov, 0), into(end_d, end_dv, 1)]
+    halves = []
+    for p in range(2):
+        part = pl.ds(4 * p, 4)
+        halves.append((p, 0, into(att.at[part], att_v.at[part], 2 + 2 * p)))
+        halves.append((p, 1, into(gq.at[part], gq_v.at[part], 3 + 2 * p)))
+    grads = [into(gk, gk_v, 6), into(gv, gv_v, 7)]
+    for copy in ends:
+        copy.wait()
+    backs = []
+
+    def back(src, dst, i):
+        copy = pltpu.make_async_copy(src, dst, back_sem.at[i])
+        copy.start()
+        backs.append(copy)
+
+    for p, w, copy in halves:
+        copy.wait()
+        part = pl.ds(4 * p, 4)
+        buffer = (att_v, gq_v)[w]
+        for r in range(4 * p, 4 * p + 4):
+            image = reads[r, block_row]
+            if w == 0:
+                block = end_ov[image % 4, image // 4]
+            else:
+                block = end_dv[image // 4, image % 4]
+            for g in range(HALF):
+                cols = pl.ds(pl.multiple_of(cols0 + g * HD, HD), HD)
+                buffer[r, :, cols] = block[g * SEG : (g + 1) * SEG, :]
+        back(buffer.at[part], (att_out, gq_out)[w].at[part], 2 * p + w)
+    for copy in grads:
+        copy.wait()
+    back(gk_v, gk_out, 4)
+    back(gv_v, gv_out, 5)
+    for copy in backs:
+        copy.wait()
 
 
 def per_device(queries, keys, values, reads, grad_out):
     q = queries.reshape(8, SEG, HQ * HD)
     g = grad_out.reshape(8, SEG, HQ * HD)
-    vmem = pl.BlockSpec(memory_space=pltpu.VMEM)
     hbm = pl.BlockSpec(memory_space=pl.ANY)
     unit = (ROWS, HD)
     results = pl.pallas_call(
@@ -429,14 +483,17 @@
             jax.ShapeDtypeStruct(q.shape, BF16),
             jax.ShapeDtypeStruct((1, 64, VT), BF16),
             jax.ShapeDtypeStruct((1, 64, VT), BF16),
+            jax.ShapeDtypeStruct((4, 4) + unit, BF16),
+            jax.ShapeDtypeStruct((4, 4) + unit, BF16),
         ),
-        in_specs=[pl.BlockSpec(memory_space=pltpu.SMEM)] + [hbm] * 4,
-        out_specs=(hbm, hbm, vmem, vmem),
-        scratch_shapes=[pltpu.SMEM((64,), jnp.int32)]
+        in_specs=[hbm] * 5,
+        out_specs=(hbm,) * 6,
+        scratch_shapes=[pltpu.SMEM((8, 128), jnp.int32), pltpu.SMEM((64,), jnp.int32)]
         + [pltpu.VMEM((8, SEG, 2 * HALF * HD), BF16)] * 2
         + [pltpu.VMEM((KVH - 1, 8, SEG, 2 * HALF * HD), BF16)] * 2
         + [pltpu.VMEM((VT, KVH * HD), BF16)] * 2
-        + [pltpu.VMEM((STEPS, 8, SEG, HALF * HD), BF16)] * 2
+        + [pltpu.VMEM((STEPS - 1, 8, SEG, HALF * HD), BF16)] * 2
+        + [pltpu.VMEM((1, 64, VT), BF16)] * 2
         + [pltpu.VMEM((STEPS, 3, 4) + unit, BF16)] * 4
         + [pltpu.VMEM((STEPS, 4, 4) + unit, BF16)] * 8
         + [pltpu.VMEM((KVH, JP, HD), BF16)] * 2
@@ -466,6 +523,8 @@
             pltpu.SemaphoreType.DMA((2,)),
             pltpu.SemaphoreType.DMA((2,)),
             pltpu.SemaphoreType.DMA((2,)),
+            pltpu.SemaphoreType.DMA((4,)),
+            pltpu.SemaphoreType.DMA,
         ],
         compiler_params=pltpu.CompilerParams(
             collective_id=0, has_side_effects=True, vmem_limit_bytes=62 * 1024 * 1024
@@ -473,12 +532,13 @@
     )(reads.T, q, g, keys, values)
     attended, grad_queries, grad_keys, grad_values = pl.pallas_call(
         copy_out,
-        out_shape=tuple(jax.ShapeDtypeStruct(r.shape, r.dtype) for r in results),
-        in_specs=[hbm] * 4,
+        out_shape=tuple(jax.ShapeDtypeStruct(r.shape, r.dtype) for r in results[:4]),
+        in_specs=[hbm] * 7,
         out_specs=(hbm,) * 4,
-        scratch_shapes=[pltpu.VMEM(r.shape, r.dtype) for r in results]
-        + [pltpu.SemaphoreType.DMA((2, 4, 2))],
-    )(*results)
+        scratch_shapes=[pltpu.SMEM((8, 128), jnp.int32)]
+        + [pltpu.VMEM(r.shape, r.dtype) for r in results]
+        + [pltpu.SemaphoreType.DMA((9,)), pltpu.SemaphoreType.DMA((6,))],
+    )(reads.T, *results)
     return (
         attended.reshape(queries.shape),
         grad_queries.reshape(queries.shape),

time: 106 us -> 104 us (0.981)
  Pallas kernels: 105 us -> 103 us
    pallas_call x1, Pallas kernels: 102 us -> 100 us  [per_device(): pl.pallas_call(kernel, out_shape=(jax.ShapeDtypeStruct(q.shape, BF16), ja...]
where the time goes in v3:
time: 104 us; the launch traced here: 103 us
  Pallas kernels  103 us (99%)
    pallas_call x1, Pallas kernels, per_device(): pl.pallas_call(kernel, out_shape=(jax.ShapeDtypeStruct(q.shape, BF16), ja...  100 us
    pallas_call x1, Pallas kernels, per_device(): pl.pallas_call(copy_out, out_shape=tuple((jax.ShapeDtypeStruct(r.shape, r...  2.8 us

profile of v3, /device:TPU:32, one launch (start us, length us, event | category | flops | bytes accessed | tf_op | source)
XLA Modules:
  0.0 103.4 jit_solution(16118411074685249834)
XLA Ops:
  0.6 100.0 %shard_map.84 = (bf16[8,16,4096]{2,1,0:T(8,128)(2,1)}, bf16[8,16,4096]{2,1,0:T(8,128)(2,1)}, bf16[1,64,1601]{2,1,0:T(8,128)(2,1)}, bf16[1,64,1601]{2,1,0:T(8,128...) custom-call(s32[8,128]{1,0:T(8,128)} %bitcast.9, bf16[8,16,4096]{2,1,0:T(8,128)(2,1)} %bitcast.7, ...), custom_call_target="tpu_custom_call" | custom-call | tf_op jit(solution)/shard_map/pallas_call | solution.py:479
  100.6 2.8 %shard_map.85 = (bf16[8,16,4096]{2,1,0:T(8,128)(2,1)}, bf16[8,16,4096]{2,1,0:T(8,128)(2,1)}, bf16[1,64,1601]{2,1,0:T(8,128)(2,1)}, bf16[1,64,1601]{2,1,0:T(8,128)(2,1)}) custom-call(s32[8,128]{1,0:T(8,128)} %bitcast.10, bf16[8,16,4096]{2,1,0:T(8,128)(2,1)} %get-tuple-element.14.att, bf16[8,16,4096]{2,1,0:T(8,128)(2,1)} %get-tuple-element.15.gq, ...), custom_call_target="tpu_custom_call" | custom-call | tf_op jit(solution)/shard_map/pallas_call | solution.py:533

commit v4 on v3

--- a/solution.py
+++ b/solution.py
@@ -17,6 +17,7 @@
 SLOTS = 12
 WIDE = SLOTS * ROWS
 VT = 1601
+VT_MAIN = 1600
 VT16 = 1616
 JP = 1664
 LOG2E = 1.4426950408889634
@@ -31,7 +32,7 @@
 
 
 def kernel(
-    reads_hbm, q_hbm, g_hbm, k_hbm, v_hbm, att_out, gq_out, gk_out, gv_out, end_o, end_d,
+    reads_hbm, q_hbm, g_hbm, k_hbm, v_hbm, k_end, v_end, att_out, gq_out, gk_out, gv_out, end_o, end_d,
     reads, tab, q_0, g_0, q_in, g_in, k_in, v_in, att_v, gq_v, gk_v, gv_v,
     a_q, a_g, a_o, a_d, m_q, m_g, m_o, m_d, r_q, r_g, r_o, r_d,
     kh, vh, kt, vt, stage_q, stage_g, pack_o, pack_d, s_scr, p_scr, k_acc, v_acc,
@@ -59,7 +60,7 @@
             src_ref=first[ten].at[s, d - 1],
             dst_ref=middle[ten].at[s, :, own[ten][0]],
             send_sem=s1.at[ten],
-            recv_sem=w1.at[ten, s],
+            recv_sem=w1.at[ten // 2, s],
             device_id=peer(ten % 2, d),
             device_id_type=MESH,
         )
@@ -94,9 +95,9 @@
         ).wait_send()
 
     def forward(pair, s):
-        for ten in pair:
-            await_recv(first[ten].at[s], w1.at[ten, s])
-            for d in (2, 1, 3):
+        await_recv(first[pair[0]].at[pl.ds(0, 2)], w1.at[pair[0] // 2, s])
+        for d in (2, 1, 3):
+            for ten in pair:
                 hop2(ten, s, d).start()
 
     def arrive(pair, s):
@@ -122,19 +123,21 @@
             return pltpu.make_async_copy(src.at[:, :, cols], (q_0, g_0)[ten], l0.at[ten])
         return pltpu.make_async_copy(src.at[:, :, cols], dst.at[t - 1], ls.at[ten])
 
+    table = pltpu.make_async_copy(reads_hbm, reads, lr)
+    table.start()
+    load(0, 0).start()
+    load(1, 0).start()
     barrier = pltpu.get_barrier_semaphore()
     for d in (1, 2, 3):
         for target in (peer(0, d), peer(1, d), (((z + d) % 4) * 2 + core, en)):
             pl.semaphore_signal(barrier, inc=1, device_id=target, device_id_type=MESH)
     pl.semaphore_signal(barrier, inc=1, device_id=(z * 2 + 1 - core, en), device_id_type=MESH)
-    table = pltpu.make_async_copy(reads_hbm, reads, lr)
-    table.start()
-    for t in range(KVH):
+    for t in range(1, KVH):
         load(0, t).start()
         load(1, t).start()
     loads_kv = [
-        pltpu.make_async_copy(k_hbm.at[0], k_in, lk.at[0]),
-        pltpu.make_async_copy(v_hbm.at[0], v_in, lk.at[1]),
+        pltpu.make_async_copy(k_hbm.at[0, pl.ds(0, VT_MAIN)], k_in, lk.at[0]),
+        pltpu.make_async_copy(v_hbm.at[0, pl.ds(0, VT_MAIN)], v_in, lk.at[1]),
     ]
     for copy in loads_kv:
         copy.start()
@@ -148,9 +151,10 @@
             found = jnp.where(own_reads[r] == image, r, found)
         tab[T_SEND + image] = found
 
-    def pack_in(s, u, sources):
+    def pack_in(s, u, sources, tens=IN):
         cols = pl.ds(pl.multiple_of(u * (HALF * HD), HALF * HD), HALF * HD)
-        for ten, src in ((0, sources[0]), (1, sources[1])):
+        for ten in tens:
+            src = sources[ten]
             a_own = own[ten][0]
             for d in range(4):
                 a = (a_own + d) % 4
@@ -167,9 +171,11 @@
 
     load(0, 0).wait()
     load(1, 0).wait()
-    pack_in(0, 0, (q_0, g_0))
+    pack_in(0, 0, (q_0, g_0), (0,))
     pl.semaphore_wait(barrier, 10)
-    start1(IN, 0)
+    start1((0,), 0)
+    pack_in(0, 0, (q_0, g_0), (1,))
+    start1((1,), 0)
     pack_in(1, 1, (q_0, g_0))
     start1(IN, 1)
     pltpu.make_async_copy(q_in, q_in, ls.at[0]).wait()
@@ -211,13 +217,12 @@
 
     def heads(t, carry):
         cols = pl.ds(pl.multiple_of(head_at(t) * HD, HD), HD)
-        for src, rows_ref, cols_ref in ((k_in, kh, kt), (v_in, vh, vt)):
-            rows_ref[t, 0:1600, :] = src[0:1600, cols]
-            tail = src[1600:VT, cols].astype(F32)
-            mark = lax.broadcasted_iota(jnp.int32, (64, HD), 0) == 0
-            rows_ref[t, 1600:JP, :] = jnp.where(
-                mark, jnp.broadcast_to(tail, (64, HD)), 0.0
-            ).astype(BF16)
+        for src, end, rows_ref, cols_ref in ((k_in, k_end, kh, kt), (v_in, v_end, vh, vt)):
+            rows_ref[t, 0:VT_MAIN, :] = src[:, cols]
+            tail = end[0, :, cols].astype(F32)
+            mark = lax.broadcasted_iota(jnp.int32, tail.shape, 0) == 0
+            rows_ref[t, VT_MAIN:VT16, :] = jnp.where(mark, tail, 0.0).astype(BF16)
+            rows_ref[t, VT16:JP, :] = jnp.zeros((JP - VT16, HD), BF16)
             for j in range(0, JP, HD):
                 cols_ref[t, :, j : j + HD] = rows_ref[t, j : j + HD, :].T
         return carry
@@ -289,8 +294,8 @@
         def _():
             forward(OUT, s - 2)
 
-        delta = jnp.sum(g_t * o_t, axis=0, keepdims=True) * inv
         g_s = (g_t * inv).astype(BF16)
+        delta = jnp.sum(g_s.astype(F32) * o_t, axis=0, keepdims=True)
         d_t = jnp.zeros((HD, WIDE), F32)
         for j, n in CHUNKS:
             dp = jnp.dot(vh[t, j : j + n, :], g_s, preferred_element_type=F32)
@@ -478,6 +483,7 @@
     unit = (ROWS, HD)
     results = pl.pallas_call(
         kernel,
+        grid=(1,),
         out_shape=(
             jax.ShapeDtypeStruct(q.shape, BF16),
             jax.ShapeDtypeStruct(q.shape, BF16),
@@ -486,12 +492,12 @@
             jax.ShapeDtypeStruct((4, 4) + unit, BF16),
             jax.ShapeDtypeStruct((4, 4) + unit, BF16),
         ),
-        in_specs=[hbm] * 5,
+        in_specs=[hbm] * 5 + [pl.BlockSpec((1, 16, KVH * HD), lambda i: (0, VT_MAIN // 16, 0))] * 2,
         out_specs=(hbm,) * 6,
         scratch_shapes=[pltpu.SMEM((8, 128), jnp.int32), pltpu.SMEM((64,), jnp.int32)]
         + [pltpu.VMEM((8, SEG, 2 * HALF * HD), BF16)] * 2
         + [pltpu.VMEM((KVH - 1, 8, SEG, 2 * HALF * HD), BF16)] * 2
-        + [pltpu.VMEM((VT, KVH * HD), BF16)] * 2
+        + [pltpu.VMEM((VT_MAIN, KVH * HD), BF16)] * 2
         + [pltpu.VMEM((STEPS - 1, 8, SEG, HALF * HD), BF16)] * 2
         + [pltpu.VMEM((1, 64, VT), BF16)] * 2
         + [pltpu.VMEM((STEPS, 3, 4) + unit, BF16)] * 4
@@ -512,7 +518,7 @@
         ]
         + [
             pltpu.SemaphoreType.DMA((4,)),
-            pltpu.SemaphoreType.DMA((4, STEPS)),
+            pltpu.SemaphoreType.DMA((2, STEPS)),
             pltpu.SemaphoreType.DMA((4,)),
             pltpu.SemaphoreType.DMA((2, STEPS)),
         ]
@@ -529,7 +535,7 @@
         compiler_params=pltpu.CompilerParams(
             collective_id=0, has_side_effects=True, vmem_limit_bytes=62 * 1024 * 1024
         ),
-    )(reads.T, q, g, keys, values)
+    )(reads.T, q, g, keys, values, keys, values)
     attended, grad_queries, grad_keys, grad_values = pl.pallas_call(
         copy_out,
         out_shape=tuple(jax.ShapeDtypeStruct(r.shape, r.dtype) for r in results[:4]),

time: 104 us -> 104 us (level)
  no operation moved by 1% of the time
where the time goes in v4:
time: 104 us; the launch traced here: 103 us
  Pallas kernels  103 us (99%)
    pallas_call x1, Pallas kernels, per_device(): pl.pallas_call(kernel, grid=(1,), out_shape=(jax.ShapeDtypeStruct(q.shape...  99.7 us
    pallas_call x1, Pallas kernels, per_device(): pl.pallas_call(copy_out, out_shape=tuple((jax.ShapeDtypeStruct(r.shape, r...  2.8 us

profile of v4, /device:TPU:32, one launch (start us, length us, event | category | flops | bytes accessed | tf_op | source)
XLA Modules:
  0.0 103.2 jit_solution(17010822333661437951)
XLA Ops:
  0.6 99.7 %shard_map.84 = (bf16[8,16,4096]{2,1,0:T(8,128)(2,1)}, bf16[8,16,4096]{2,1,0:T(8,128)(2,1)}, bf16[1,64,1601]{2,1,0:T(8,128)(2,1)}, bf16[1,64,1601]{2,1,0:T(8,128...) custom-call(s32[8,128]{1,0:T(8,128)} %bitcast.9, bf16[8,16,4096]{2,1,0:T(8,128)(2,1)} %bitcast.7, ...), custom_call_target="tpu_custom_call" | custom-call | tf_op jit(solution)/shard_map/pallas_call | solution.py:484
  100.4 2.8 %shard_map.85 = (bf16[8,16,4096]{2,1,0:T(8,128)(2,1)}, bf16[8,16,4096]{2,1,0:T(8,128)(2,1)}, bf16[1,64,1601]{2,1,0:T(8,128)(2,1)}, bf16[1,64,1601]{2,1,0:T(8,128)(2,1)}) custom-call(s32[8,128]{1,0:T(8,128)} %bitcast.10, bf16[8,16,4096]{2,1,0:T(8,128)(2,1)} %get-tuple-element.14.att, bf16[8,16,4096]{2,1,0:T(8,128)(2,1)} %get-tuple-element.15.gq, ...), custom_call_target="tpu_custom_call" | custom-call | tf_op jit(solution)/shard_map/pallas_call | solution.py:539

commit v5 on v4

--- a/solution.py
+++ b/solution.py
@@ -32,12 +32,12 @@
 
 
 def kernel(
-    reads_hbm, q_hbm, g_hbm, k_hbm, v_hbm, k_end, v_end, att_out, gq_out, gk_out, gv_out, end_o, end_d,
-    reads, tab, q_0, g_0, q_in, g_in, k_in, v_in, att_v, gq_v, gk_v, gv_v,
+    reads_hbm, q_hbm, g_hbm, k_in, v_in, att_out, gq_out, gk_out, gv_out, end_o, end_d,
+    reads, tab, q_0, g_0, q_in, g_in, att_v, gq_v, gk_v, gv_v,
     a_q, a_g, a_o, a_d, m_q, m_g, m_o, m_d, r_q, r_g, r_o, r_d,
     kh, vh, kt, vt, stage_q, stage_g, pack_o, pack_d, s_scr, p_scr, k_acc, v_acc,
     z_send, z_recv, c_send, c_recv,
-    s1, w1, s2, w2, zs, zw, cs, cw, l0, ls, lo, lk, le, lr,
+    s1, w1, s2, w2, zs, zw, cs, cw, l0, ls, lo, le, lr,
 ):
     sq = lax.axis_index("seq")
     en = lax.axis_index("enc")
@@ -135,13 +135,6 @@
     for t in range(1, KVH):
         load(0, t).start()
         load(1, t).start()
-    loads_kv = [
-        pltpu.make_async_copy(k_hbm.at[0, pl.ds(0, VT_MAIN)], k_in, lk.at[0]),
-        pltpu.make_async_copy(v_hbm.at[0, pl.ds(0, VT_MAIN)], v_in, lk.at[1]),
-    ]
-    for copy in loads_kv:
-        copy.start()
-
     block_row = sq * 16 + en
     table.wait()
     own_reads = [reads[r, block_row] for r in range(8)]
@@ -212,17 +205,15 @@
     forward(IN, 0)
     start1(IN, AHEAD)
 
-    for copy in loads_kv:
-        copy.wait()
-
     def heads(t, carry):
         cols = pl.ds(pl.multiple_of(head_at(t) * HD, HD), HD)
-        for src, end, rows_ref, cols_ref in ((k_in, k_end, kh, kt), (v_in, v_end, vh, vt)):
-            rows_ref[t, 0:VT_MAIN, :] = src[:, cols]
-            tail = end[0, :, cols].astype(F32)
-            mark = lax.broadcasted_iota(jnp.int32, tail.shape, 0) == 0
-            rows_ref[t, VT_MAIN:VT16, :] = jnp.where(mark, tail, 0.0).astype(BF16)
-            rows_ref[t, VT16:JP, :] = jnp.zeros((JP - VT16, HD), BF16)
+        for src, rows_ref, cols_ref in ((k_in, kh, kt), (v_in, vh, vt)):
+            rows_ref[t, 0:VT_MAIN, :] = src[0, 0:VT_MAIN, cols]
+            tail = src[0, VT_MAIN:VT, cols].astype(F32)
+            mark = lax.broadcasted_iota(jnp.int32, (64, HD), 0) == 0
+            rows_ref[t, VT_MAIN:JP, :] = jnp.where(
+                mark, jnp.broadcast_to(tail, (64, HD)), 0.0
+            ).astype(BF16)
             for j in range(0, JP, HD):
                 cols_ref[t, :, j : j + HD] = rows_ref[t, j : j + HD, :].T
         return carry
@@ -483,7 +474,6 @@
     unit = (ROWS, HD)
     results = pl.pallas_call(
         kernel,
-        grid=(1,),
         out_shape=(
             jax.ShapeDtypeStruct(q.shape, BF16),
             jax.ShapeDtypeStruct(q.shape, BF16),
@@ -492,12 +482,11 @@
             jax.ShapeDtypeStruct((4, 4) + unit, BF16),
             jax.ShapeDtypeStruct((4, 4) + unit, BF16),
         ),
-        in_specs=[hbm] * 5 + [pl.BlockSpec((1, 16, KVH * HD), lambda i: (0, VT_MAIN // 16, 0))] * 2,
+        in_specs=[hbm] * 3 + [pl.BlockSpec(memory_space=pltpu.VMEM)] * 2,
         out_specs=(hbm,) * 6,
         scratch_shapes=[pltpu.SMEM((8, 128), jnp.int32), pltpu.SMEM((64,), jnp.int32)]
         + [pltpu.VMEM((8, SEG, 2 * HALF * HD), BF16)] * 2
         + [pltpu.VMEM((KVH - 1, 8, SEG, 2 * HALF * HD), BF16)] * 2
-        + [pltpu.VMEM((VT_MAIN, KVH * HD), BF16)] * 2
         + [pltpu.VMEM((STEPS - 1, 8, SEG, HALF * HD), BF16)] * 2
         + [pltpu.VMEM((1, 64, VT), BF16)] * 2
         + [pltpu.VMEM((STEPS, 3, 4) + unit, BF16)] * 4
@@ -528,14 +517,13 @@
             pltpu.SemaphoreType.DMA((2,)),
             pltpu.SemaphoreType.DMA((2,)),
             pltpu.SemaphoreType.DMA((2,)),
-            pltpu.SemaphoreType.DMA((2,)),
             pltpu.SemaphoreType.DMA((4,)),
             pltpu.SemaphoreType.DMA,
         ],
         compiler_params=pltpu.CompilerParams(
             collective_id=0, has_side_effects=True, vmem_limit_bytes=62 * 1024 * 1024
         ),
-    )(reads.T, q, g, keys, values, keys, values)
+    )(reads.T, q, g, keys, values)
     attended, grad_queries, grad_keys, grad_values = pl.pallas_call(
         copy_out,
         out_shape=tuple(jax.ShapeDtypeStruct(r.shape, r.dtype) for r in results[:4]),

time: 104 us -> 105 us (level)
    pallas_call x1, Pallas kernels: 99.7 us -> 101 us  [per_device(): pl.pallas_call(kernel, out_shape=(jax.ShapeDtypeStruct(q.shape, BF16), ja...]
where the time goes in v5:
time: 105 us; the launch traced here: 104 us
  Pallas kernels  104 us (99%)
    pallas_call x1, Pallas kernels, per_device(): pl.pallas_call(kernel, out_shape=(jax.ShapeDtypeStruct(q.shape, BF16), ja...  101 us
    pallas_call x1, Pallas kernels, per_device(): pl.pallas_call(copy_out, out_shape=tuple((jax.ShapeDtypeStruct(r.shape, r...  2.8 us

profile of v5, /device:TPU:32, one launch (start us, length us, event | category | flops | bytes accessed | tf_op | source)
XLA Modules:
  0.0 104.4 jit_solution(7070467840051806754)
XLA Ops:
  0.6 100.9 %shard_map.84 = (bf16[8,16,4096]{2,1,0:T(8,128)(2,1)}, bf16[8,16,4096]{2,1,0:T(8,128)(2,1)}, bf16[1,64,1601]{2,1,0:T(8,128)(2,1)}, bf16[1,64,1601]{2,1,0:T(8,128...) custom-call(s32[8,128]{1,0:T(8,128)} %bitcast.9, bf16[8,16,4096]{2,1,0:T(8,128)(2,1)} %bitcast.7, ...), custom_call_target="tpu_custom_call" | custom-call | tf_op jit(solution)/shard_map/pallas_call | solution.py:475
  101.6 2.8 %shard_map.85 = (bf16[8,16,4096]{2,1,0:T(8,128)(2,1)}, bf16[8,16,4096]{2,1,0:T(8,128)(2,1)}, bf16[1,64,1601]{2,1,0:T(8,128)(2,1)}, bf16[1,64,1601]{2,1,0:T(8,128)(2,1)}) custom-call(s32[8,128]{1,0:T(8,128)} %bitcast.10, bf16[8,16,4096]{2,1,0:T(8,128)(2,1)} %get-tuple-element.14.att, bf16[8,16,4096]{2,1,0:T(8,128)(2,1)} %get-tuple-element.15.gq, ...), custom_call_target="tpu_custom_call" | custom-call | tf_op jit(solution)/shard_map/pallas_call | solution.py:527

commit v6 on v4

--- a/solution.py
+++ b/solution.py
@@ -123,15 +123,19 @@
             return pltpu.make_async_copy(src.at[:, :, cols], (q_0, g_0)[ten], l0.at[ten])
         return pltpu.make_async_copy(src.at[:, :, cols], dst.at[t - 1], ls.at[ten])
 
+    barrier = pltpu.get_barrier_semaphore()
+    for d in (2, 1, 3):
+        pl.semaphore_signal(
+            barrier, inc=1, device_id=(((z + d) % 4) * 2 + core, en), device_id_type=MESH
+        )
+    for d in (2, 1, 3):
+        for target in (peer(0, d), peer(1, d)):
+            pl.semaphore_signal(barrier, inc=1, device_id=target, device_id_type=MESH)
+    pl.semaphore_signal(barrier, inc=1, device_id=(z * 2 + 1 - core, en), device_id_type=MESH)
     table = pltpu.make_async_copy(reads_hbm, reads, lr)
     table.start()
     load(0, 0).start()
     load(1, 0).start()
-    barrier = pltpu.get_barrier_semaphore()
-    for d in (1, 2, 3):
-        for target in (peer(0, d), peer(1, d), (((z + d) % 4) * 2 + core, en)):
-            pl.semaphore_signal(barrier, inc=1, device_id=target, device_id_type=MESH)
-    pl.semaphore_signal(barrier, inc=1, device_id=(z * 2 + 1 - core, en), device_id_type=MESH)
     for t in range(1, KVH):
         load(0, t).start()
         load(1, t).start()

time: 104 us -> 104 us (level)
  no operation moved by 1% of the time
where the time goes in v6:
time: 104 us
  Pallas kernels  103 us (99%)
    pallas_call x1, Pallas kernels, per_device(): pl.pallas_call(kernel, grid=(1,), out_shape=(jax.ShapeDtypeStruct(q.shape...  100 us
    pallas_call x1, Pallas kernels, per_device(): pl.pallas_call(copy_out, out_shape=tuple((jax.ShapeDtypeStruct(r.shape, r...  2.8 us

profile of v6, /device:TPU:32, one launch (start us, length us, event | category | flops | bytes accessed | tf_op | source)
XLA Modules:
  0.0 103.9 jit_solution(8745631723891669612)
XLA Ops:
  0.6 100.4 %shard_map.84 = (bf16[8,16,4096]{2,1,0:T(8,128)(2,1)}, bf16[8,16,4096]{2,1,0:T(8,128)(2,1)}, bf16[1,64,1601]{2,1,0:T(8,128)(2,1)}, bf16[1,64,1601]{2,1,0:T(8,128...) custom-call(s32[8,128]{1,0:T(8,128)} %bitcast.9, bf16[8,16,4096]{2,1,0:T(8,128)(2,1)} %bitcast.7, ...), custom_call_target="tpu_custom_call" | custom-call | tf_op jit(solution)/shard_map/pallas_call | solution.py:488
  101.1 2.8 %shard_map.85 = (bf16[8,16,4096]{2,1,0:T(8,128)(2,1)}, bf16[8,16,4096]{2,1,0:T(8,128)(2,1)}, bf16[1,64,1601]{2,1,0:T(8,128)(2,1)}, bf16[1,64,1601]{2,1,0:T(8,128)(2,1)}) custom-call(s32[8,128]{1,0:T(8,128)} %bitcast.10, bf16[8,16,4096]{2,1,0:T(8,128)(2,1)} %get-tuple-element.14.att, bf16[8,16,4096]{2,1,0:T(8,128)(2,1)} %get-tuple-element.15.gq, ...), custom_call_target="tpu_custom_call" | custom-call | tf_op jit(solution)/shard_map/pallas_call | solution.py:543
